TPU v7x, 32 devices: a whole 2x2x4 slice. The times are simulated.
32 devices in a mesh: elec: 8 (over z, y), space: 4 (over x, core).
Axes of the slice: x: 2, y: 2, z: 4, core: 2. Of those that a mesh axis runs over, the one named last changes fastest.
Arguments:
- sigma_real: float32 [8, 64, 128], P('space'), may hold values from 0.3 to 3
- sigma_imag: float32 [8, 64, 128], P('space'), may hold values from -0.5 to 0.5
- warm_fields: float32 [32, 2, 8, 64, 128], P('elec', None, 'space'), may hold values from -6 to 6
- locations: int32 [32], P('elec'), may hold values from 0 to 65535
- counts: int32 [8], P('elec'), may hold values from 1 to 48, 128 in all
- quads: int32 [8, 48, 4], P('elec'), may hold values from 0 to 31
Outputs:
- jacobian: bfloat16 [128, 2, 8, 64, 128], P('elec', None, 'space')
Inputs may be any that keep to these rules, and one draw needn't show every extreme that they name: The counts sum to 128; group h's measurements are its first counts[h] slots. `quads`: slots past a group's count are unused.
All inputs are finite; a program needn't handle non-finite values.
Results may differ from a plain program's by a relative error of at most 0.0072.
Values may be sent and summed in bfloat16 or wider, within the bound.
A program may use at most 128 MiB of HBM per device.

v0:
```python
import math

import jax
import jax.numpy as jnp
from jax import lax
from jax.sharding import PartitionSpec as P

MEASURE_ROWS_MEAN = 16
ITERS = 2


screen = 0.3
current = 4.0


def padded_2(cells, sides, width):
    for axis, dim in sides:
        count = lax.axis_size(axis)
        ends = count - 1
        head = lax.slice_in_dim(cells, 0, width, axis=dim)
        tail = lax.slice_in_dim(cells, cells.shape[dim] - width, cells.shape[dim], axis=dim)
        cells = jnp.concatenate(
            [
                lax.ppermute(tail, axis, [(i, (i + 1) % count) for i in range(ends)]),
                cells,
                lax.ppermute(head, axis, [((i + 1) % count, i) for i in range(ends)]),
            ],
            axis=dim,
        )
    return cells


def relax_weights(count):
    spread_half = 6.0 / (6.0 + screen)
    return [
        1.0 / (1.0 + spread_half * math.cos(math.pi * (2 * k + 1) / (2 * count)))
        for k in range(count)
    ]


def gradients_of(padded_potential):
    values = padded_potential.astype(jnp.float32)
    interior = values[:, :, 1:-1]
    grad_x = (values[:, :, 2:] - values[:, :, :-2]) * 0.5
    side_pad = jnp.pad(interior, ((0, 0), (0, 0), (0, 0), (1, 1), (1, 1)))
    grad_y = (side_pad[:, :, :, 2:, 1:-1] - side_pad[:, :, :, :-2, 1:-1]) * 0.5
    grad_z = (side_pad[:, :, :, 1:-1, 2:] - side_pad[:, :, :, 1:-1, :-2]) * 0.5
    return jnp.stack([grad_x, grad_y, grad_z], axis=2).astype(jnp.bfloat16)


def per_device(sigma_real, sigma_imag, warm_fields, locations, counts, quads):
    group_width, cells_along_y, cells_along_z = sigma_real.shape
    slab = lax.axis_index("space")
    x_global = slab * group_width + lax.broadcasted_iota(
        jnp.int32, (group_width, cells_along_y, cells_along_z), 0
    )
    y_index = lax.broadcasted_iota(jnp.int32, (group_width, cells_along_y, cells_along_z), 1)
    z_index = lax.broadcasted_iota(jnp.int32, (group_width, cells_along_y, cells_along_z), 2)
    flat_index = (x_global * cells_along_y + y_index) * cells_along_z + z_index
    inverse = 1.0 / ((6.0 + screen) * (sigma_real * sigma_real + sigma_imag * sigma_imag))
    strength = jnp.where(
        flat_index[None] == locations[:, None, None, None], jnp.float32(current), jnp.float32(0.0)
    )
    source = jnp.stack(
        [strength * sigma_real * inverse, -(strength * sigma_imag * inverse)], axis=1
    )
    weights = relax_weights(ITERS)
    field = warm_fields
    for iteration in range(ITERS):
        padded = padded_2(field, (("space", 2),), 1)
        interior = padded[:, :, 1:-1]
        side_pad = jnp.pad(interior, ((0, 0), (0, 0), (0, 0), (1, 1), (1, 1)))
        total = padded[:, :, 2:] + padded[:, :, :-2]
        total = total + side_pad[:, :, :, 2:, 1:-1] + side_pad[:, :, :, :-2, 1:-1]
        total = total + side_pad[:, :, :, 1:-1, 2:] + side_pad[:, :, :, 1:-1, :-2]
        field = field + weights[iteration] * (source - field + total / (6.0 + screen))
    potential = field.astype(jnp.bfloat16)
    own_grads = gradients_of(padded_2(potential, (("space", 2),), 1))
    gradient_table = lax.all_gather(own_grads, "elec", axis=0, tiled=True)
    all_counts, all_quads = (
        lax.all_gather(counts, "elec", axis=0, tiled=True),
        lax.all_gather(quads, "elec", axis=0, tiled=True),
    )
    capacity = all_quads.shape[1]
    ends = jnp.cumsum(all_counts)
    starts = ends - all_counts
    measure_group = lax.axis_index("elec")
    row_indices = measure_group * MEASURE_ROWS_MEAN + jnp.arange(MEASURE_ROWS_MEAN, dtype=jnp.int32)
    owners = jnp.sum((ends[None, :] <= row_indices[:, None]).astype(jnp.int32), axis=1)
    slot_ids = row_indices - starts[owners]
    chosen = all_quads.reshape(-1, 4)[owners * capacity + slot_ids]
    electrodes = gradient_table.shape[0]
    electrode_ids = jnp.arange(electrodes, dtype=jnp.int32)[None, :]
    select_source = (chosen[:, 0:1] == electrode_ids).astype(jnp.float32) - (
        chosen[:, 1:2] == electrode_ids
    ).astype(jnp.float32)
    select_probe = (chosen[:, 2:3] == electrode_ids).astype(jnp.float32) - (
        chosen[:, 3:4] == electrode_ids
    ).astype(jnp.float32)
    selector = jnp.concatenate([select_source, select_probe], axis=0).astype(jnp.bfloat16)
    field_products = jnp.dot(
        selector, gradient_table.reshape(electrodes, -1), preferred_element_type=jnp.float32
    )
    field_products = field_products.reshape(
        2, MEASURE_ROWS_MEAN, 2, 3, group_width, cells_along_y, cells_along_z
    )
    pair_source = field_products[0]
    pair_probe = field_products[1]
    dot_real = jnp.sum(
        pair_source[:, 0] * pair_probe[:, 0] - pair_source[:, 1] * pair_probe[:, 1], axis=1
    )
    dot_imag = jnp.sum(
        pair_source[:, 0] * pair_probe[:, 1] + pair_source[:, 1] * pair_probe[:, 0], axis=1
    )
    part_real = -(sigma_real * dot_real - sigma_imag * dot_imag)
    part_imag = -(sigma_real * dot_imag + sigma_imag * dot_real)
    return jnp.stack([part_real, part_imag], axis=1).astype(jnp.bfloat16)


def solution(mesh):
    in_specs = (
        P("space", None, None),
        P("space", None, None),
        P("elec", None, "space", None, None),
        P("elec"),
        P("elec"),
        P("elec", None, None),
    )
    out_specs = P("elec", None, "space", None, None)
    return jax.shard_map(
        per_device, mesh=mesh, in_specs=in_specs, out_specs=out_specs, check_vma=False
    )
```

profile of v0, /device:TPU:2, one launch (start us, length us, event | category | flops | bytes accessed | tf_op | source)
XLA Modules:
  0.0 177.1 jit_solution(6735330070216509067)
XLA Ops:
  6.5 1.1 fusion.50
  7.6 1.9 %collective-permute-start = (f32[4,2,1,64,128]{4,3,2,1,0:T(8,128)S(1)}, f32[4,2,1,64,128]{4,3,2,1,0:T(8,128)S(1)}, u32[]{:S(2)}, u32[]{:S(2)}) collective-permute-start(f32[4,2,1,64,128]{4,3,2,1,0:T(8,128)S(1)} %get-tuple-element.21), channel_id=1, source_target_pairs={{1,0},{2,1},{3,2},{5,4},{6,5},{7,6},{9,8},{10,9},{11,10},{13,12},{... | collective-permute-start | bytes 786440 | tf_op jit(solution)/shard_map/ppermute | solution.py:26
  9.5 2.4 %collective-permute-start.1 = (f32[4,2,1,64,128]{4,3,2,1,0:T(8,128)S(1)}, f32[4,2,1,64,128]{4,3,2,1,0:T(8,128)S(1)}, u32[]{:S(2)}, u32[]{:S(2)}) collective-permute-start(f32[4,2,1,64,128]{4,3,2,1,0:T(8,128)S(1)} %get-tuple-element.22), channel_id=1, source_target_pairs={{0,1},{1,2},{2,3},{4,5},{5,6},{6,7},{8,9},{9,10},{10,11},{12,13},{... | collective-permute-start | bytes 786440 | tf_op jit(solution)/shard_map/ppermute | solution.py:24
  12.0 0.9 multiply_divide_fusion
  13.0 1.0 fusion.36
  14.0 3.2 %collective-permute-done.1 = f32[4,2,1,64,128]{4,3,2,1,0:T(8,128)S(1)} collective-permute-done((f32[4,2,1,64,128]{4,3,2,1,0:T(8,128)S(1)}, f32[4,2,1,64,128]{4,3,2,1,0:T(8,128)S(1)}, u32[]{:S(2)}, u32[]{:S(2)}) %collective-permute-start.1) | collective-permute-done | bytes 262176 | tf_op jit(solution)/shard_map/ppermute | solution.py:24
  17.2 3.0 %fusion.16 = f32[4,2,2,64,128]{4,3,2,1,0:T(8,128)S(1)} fusion(f32[4,2,2,64,128]{4,3,2,1,0:T(8,128)} %param.8, f32[4,2,1,64,128]{4,3,2,1,0:T(8,128)S(1)} %collective-permute-done.1, f32[4,2,1,64,128]{4,3,2,1,0:T(8,128)S(1)} %collective-permute-done, f32[4,1,2,64,128]{4,3,2,1,0:T(8,128)S(1)} %get-tuple-element.26, f32[4,1,2,64,128]{4,3,2,1,0:T(8,128)S(1)} %get-tuple-element.25), kind=kLoop, calls=%fused_computation.40 | loop fusion | flops 1703936 | bytes 2097152 | tf_op jit(solution)/shard_map/add | solution.py:76
  20.3 1.9 %collective-permute-start.2 = (f32[4,2,1,64,128]{4,3,2,1,0:T(8,128)S(1)}, f32[4,2,1,64,128]{4,3,2,1,0:T(8,128)S(1)}, u32[]{:S(2)}, u32[]{:S(2)}) collective-permute-start(f32[4,2,1,64,128]{4,3,2,1,0:T(8,128)S(1)} %get-tuple-element.19), channel_id=1, source_target_pairs={{1,0},{2,1},{3,2},{5,4},{6,5},{7,6},{9,8},{10,9},{11,10},{13,12},{... | collective-permute-start | bytes 786440 | tf_op jit(solution)/shard_map/ppermute | solution.py:26
  22.2 2.4 %collective-permute-start.3 = (f32[4,2,1,64,128]{4,3,2,1,0:T(8,128)S(1)}, f32[4,2,1,64,128]{4,3,2,1,0:T(8,128)S(1)}, u32[]{:S(2)}, u32[]{:S(2)}) collective-permute-start(f32[4,2,1,64,128]{4,3,2,1,0:T(8,128)S(1)} %get-tuple-element.20), channel_id=1, source_target_pairs={{0,1},{1,2},{2,3},{4,5},{5,6},{6,7},{8,9},{9,10},{10,11},{12,13},{... | collective-permute-start | bytes 786440 | tf_op jit(solution)/shard_map/ppermute | solution.py:24
  24.7 1.4 collective-permute-done.2
  26.1 3.8 %collective-permute-done.3 = f32[4,2,1,64,128]{4,3,2,1,0:T(8,128)S(1)} collective-permute-done((f32[4,2,1,64,128]{4,3,2,1,0:T(8,128)S(1)}, f32[4,2,1,64,128]{4,3,2,1,0:T(8,128)S(1)}, u32[]{:S(2)}, u32[]{:S(2)}) %collective-permute-start.3) | collective-permute-done | bytes 262176 | tf_op jit(solution)/shard_map/ppermute | solution.py:24
  29.9 0.5 fusion.25
  30.4 1.9 %collective-permute-start.4 = (bf16[4,2,1,64,128]{4,3,2,1,0:T(8,128)(2,1)S(1)}, bf16[4,2,1,64,128]{4,3,2,1,0:T(8,128)(2,1)S(1)}, u32[]{:S(2)}, u32[]{:S(2)}) collective-permute-start(bf16[4,2,1,64,128]{4,3,2,1,0:T(8,128)(2,1)S(1)} %get-tuple-element.23), channel_id=1, source_target_pairs={{0,1},{1,2},{2,3},{4,5},{5,6},{6,7},{8,9},{9,10},{10,11},{12,13},{... | collective-permute-start | bytes 393224 | tf_op jit(solution)/shard_map/ppermute | solution.py:24
  32.3 3.6 %collective-permute-start.5 = (bf16[4,2,1,64,128]{4,3,2,1,0:T(8,128)(2,1)S(1)}, bf16[4,2,1,64,128]{4,3,2,1,0:T(8,128)(2,1)S(1)}, u32[]{:S(2)}, u32[]{:S(2)}) collective-permute-start(bf16[4,2,1,64,128]{4,3,2,1,0:T(8,128)(2,1)S(1)} %get-tuple-element.24), channel_id=1, source_target_pairs={{1,0},{2,1},{3,2},{5,4},{6,5},{7,6},{9,8},{10,9},{11,10},{13,12},{... | collective-permute-start | bytes 393224 | tf_op jit(solution)/shard_map/ppermute | solution.py:26
  36.0 0.7 collective-permute-done.4
  36.7 1.8 %collective-permute-done.5 = bf16[4,2,1,64,128]{4,3,2,1,0:T(8,128)(2,1)S(1)} collective-permute-done((bf16[4,2,1,64,128]{4,3,2,1,0:T(8,128)(2,1)S(1)}, bf16[4,2,1,64,128]{4,3,2,1,0:T(8,128)(2,1)S(1)}, u32[]{:S(2)}, u32[]{:S(2)}) %collective-permute-start.5) | collective-permute-done | bytes 131104 | tf_op jit(solution)/shard_map/ppermute | solution.py:26
  38.7 0.4 fusion.41
  39.1 1.0 pad_maximum_fusion.1
  40.8 0.6 dynamic-slice
  41.3 0.7 dynamic-update-slice
  42.0 11.7 %all-reduce.3 = s32[8]{0:T(128)S(1)} all-reduce(s32[8]{0:T(128)S(1)} %dynamic-update-slice), channel_id=1, replica_groups=mesh['elec'=8,'space'=4] {'elec'}, use_global_device_ids=true, to_apply=%add.3 | all-reduce | flops 8 | bytes 64
  53.9 26.7 %all_gather.9 = s32[8,48,4]{1,2,0:T(4,128)S(1)} all-gather(s32[1,48,4]{1,2,0:T(4,128)S(1)} %copy-done.2), channel_id=1, replica_groups=mesh['elec'=8,'space'=4] {'elec'}, dimensions={0}, use_global_device_ids=true | all-gather | bytes 6912 | tf_op jit(solution)/shard_map/all_gather | solution.py:82
  80.8 0.7 gather_fusion
  81.5 0.6 gather_fusion.1
  82.4 58.9 %all-gather.2.cloned.1.call-done = bf16[32,2,3,2,64,128]{5,4,3,1,0,2:T(8,128)(2,1)} async-done(((bf16[4,2,3,2,64,128]{5,4,3,1,0,2:T(8,128)(2,1)}), bf16[32,2,3,2,64,128]{5,4,3,1,0,2:T(8,128)(2,1)}) %all-gather.2.cloned.1.call-update) | async-done | bytes 6291472 | tf_op jit(solution)/shard_map/all_gather | solution.py:79
  141.3 4.3 %copy.13 = bf16[32,2,3,2,64,128]{5,4,3,2,1,0:T(8,128)(2,1)S(1)} copy(bf16[32,2,3,2,64,128]{5,4,3,1,0,2:T(8,128)(2,1)} %all-gather.2.cloned.1.call-done) | data formatting | bytes 12582912 | tf_op jit(solution)/shard_map/all_gather | solution.py:79
  145.6 8.3 %fusion = f32[32,98304]{1,0:T(8,128)} fusion(bf16[4,8,768,128]{3,2,1,0:T(8,128)(2,1)S(1)} %bitcast.61, bf16[16,32]{1,0:T(8,128)(2,1)S(1)} %get-tuple-element.27, bf16[16,32]{1,0:T(8,128)(2,1)S(1)} %get-tuple-element.28), kind=kOutput, calls=%fused_computation.2 | convolution fusion | flops 201330688 | bytes 18876416 | tf_op jit(solution)/shard_map/dot_general | solution.py:101
  153.9 8.0 %slice_bitcast_fusion.1 = (f32[2,8,768,128]{3,1,2,0:T(8,128)}, f32[2,8,768,128]{3,1,2,0:T(8,128)S(1)}) fusion(f32[32,98304]{1,0:T(8,128)} %fusion), kind=kLoop, calls=%fused_computation.6 | loop fusion | bytes 25165824
  161.9 4.0 %copy.15 = f32[2,8,768,128]{3,2,1,0:T(8,128)S(1)} copy(f32[2,8,768,128]{3,1,2,0:T(8,128)} %get-tuple-element.11) | data formatting | bytes 12582912
  165.9 1.2 copy.16
  167.2 1.7 subtract_reduce_fusion
  169.2 1.1 pad_maximum_fusion
  (30 shorter events, 1.5 us)
Async XLA Ops:
  6.5 134.7 %all-gather.2.cloned.1.call-start = ((), (), s32[]{:S(2)}) async-start(), calls=%async_computation | async-start | bytes 7077888 | tf_op jit(solution)/shard_map/all_gather | solution.py:79
  7.6 6.4 %collective-permute-start = (f32[4,2,1,64,128]{4,3,2,1,0:T(8,128)S(1)}, f32[4,2,1,64,128]{4,3,2,1,0:T(8,128)S(1)}, u32[]{:S(2)}, u32[]{:S(2)}) collective-permute-start(f32[4,2,1,64,128]{4,3,2,1,0:T(8,128)S(1)} %get-tuple-element.21), channel_id=1, source_target_pairs={{1,0},{2,1},{3,2},{5,4},{6,5},{7,6},{9,8},{10,9},{11,10},{13,12},{... | collective-permute-start | bytes 786440 | tf_op jit(solution)/shard_map/ppermute | solution.py:26
  9.5 7.7 %collective-permute-start.1 = (f32[4,2,1,64,128]{4,3,2,1,0:T(8,128)S(1)}, f32[4,2,1,64,128]{4,3,2,1,0:T(8,128)S(1)}, u32[]{:S(2)}, u32[]{:S(2)}) collective-permute-start(f32[4,2,1,64,128]{4,3,2,1,0:T(8,128)S(1)} %get-tuple-element.22), channel_id=1, source_target_pairs={{0,1},{1,2},{2,3},{4,5},{5,6},{6,7},{8,9},{9,10},{10,11},{12,13},{... | collective-permute-start | bytes 786440 | tf_op jit(solution)/shard_map/ppermute | solution.py:24
  17.2 23.5 %copy-start.3 = (u32[32]{0:T(128)S(1)}, u32[32]{0:T(128)}, u32[]{:S(2)}) copy-start(u32[32]{0:T(128)} %constant.62) | copy-start | bytes 388
  17.2 36.7 %copy-start.2 = (s32[1,48,4]{1,2,0:T(4,128)S(1)}, s32[1,48,4]{1,2,0:T(4,128)}, u32[]{:S(2)}) copy-start(s32[1,48,4]{1,2,0:T(4,128)} %param.11) | copy-start | bytes 2308
  20.3 5.8 %collective-permute-start.2 = (f32[4,2,1,64,128]{4,3,2,1,0:T(8,128)S(1)}, f32[4,2,1,64,128]{4,3,2,1,0:T(8,128)S(1)}, u32[]{:S(2)}, u32[]{:S(2)}) collective-permute-start(f32[4,2,1,64,128]{4,3,2,1,0:T(8,128)S(1)} %get-tuple-element.19), channel_id=1, source_target_pairs={{1,0},{2,1},{3,2},{5,4},{6,5},{7,6},{9,8},{10,9},{11,10},{13,12},{... | collective-permute-start | bytes 786440 | tf_op jit(solution)/shard_map/ppermute | solution.py:26
  22.2 7.7 %collective-permute-start.3 = (f32[4,2,1,64,128]{4,3,2,1,0:T(8,128)S(1)}, f32[4,2,1,64,128]{4,3,2,1,0:T(8,128)S(1)}, u32[]{:S(2)}, u32[]{:S(2)}) collective-permute-start(f32[4,2,1,64,128]{4,3,2,1,0:T(8,128)S(1)} %get-tuple-element.20), channel_id=1, source_target_pairs={{0,1},{1,2},{2,3},{4,5},{5,6},{6,7},{8,9},{9,10},{10,11},{12,13},{... | collective-permute-start | bytes 786440 | tf_op jit(solution)/shard_map/ppermute | solution.py:24
  30.4 6.3 %collective-permute-start.4 = (bf16[4,2,1,64,128]{4,3,2,1,0:T(8,128)(2,1)S(1)}, bf16[4,2,1,64,128]{4,3,2,1,0:T(8,128)(2,1)S(1)}, u32[]{:S(2)}, u32[]{:S(2)}) collective-permute-start(bf16[4,2,1,64,128]{4,3,2,1,0:T(8,128)(2,1)S(1)} %get-tuple-element.23), channel_id=1, source_target_pairs={{0,1},{1,2},{2,3},{4,5},{5,6},{6,7},{8,9},{9,10},{10,11},{12,13},{... | collective-permute-start | bytes 393224 | tf_op jit(solution)/shard_map/ppermute | solution.py:24
  32.3 6.1 %collective-permute-start.5 = (bf16[4,2,1,64,128]{4,3,2,1,0:T(8,128)(2,1)S(1)}, bf16[4,2,1,64,128]{4,3,2,1,0:T(8,128)(2,1)S(1)}, u32[]{:S(2)}, u32[]{:S(2)}) collective-permute-start(bf16[4,2,1,64,128]{4,3,2,1,0:T(8,128)(2,1)S(1)} %get-tuple-element.24), channel_id=1, source_target_pairs={{1,0},{2,1},{3,2},{5,4},{6,5},{7,6},{9,8},{10,9},{11,10},{13,12},{... | collective-permute-start | bytes 393224 | tf_op jit(solution)/shard_map/ppermute | solution.py:26
  167.1 1.7 copy-start
  167.1 1.7 copy-start.1
Sparse Core Ops, SparseCore 0:
  40.2 101.0 all-gather.1
where the time goes:
time: 179 us; the launch traced here: 177 us
  waiting for transfers between devices  69.9 us (39%)
  blocking collectives  38.4 us (21%)
  local copies, waits for them, and re-layouts  21.5 us (12%)
  between operations  14.3 us (8%)
  starting transfers between devices  14.2 us (8%)
  other arithmetic  10.5 us (6%)
  matrix products  8.32 us (5%)
    all_gather x1, waiting for transfers between devices, per_device(): gradient_table = lax.all_gather(own_grads, 'elec', axis=0, tiled=True)  58.9 us
    all_gather x1, blocking collectives, per_device(): lax.all_gather(quads, 'elec', axis=0, tiled=True)  26.7 us
    unnamed x14, local copies, waits for them, and re-layouts  14.5 us
    unnamed x1, blocking collectives  11.7 us
    dot_general x1, matrix products, per_device(): jnp.dot(selector, gradient_table.reshape(electrodes, -1), preferred_eleme...  8.32 us
    ppermute x3, waiting for transfers between devices, padded_2(): lax.ppermute(tail, axis, [(i, (i + 1) % count) for i in range(ends)])  7.76 us
    ppermute x3, starting transfers between devices, padded_2(): lax.ppermute(head, axis, [((i + 1) % count, i) for i in range(ends)])  7.48 us
    ppermute x3, starting transfers between devices, padded_2(): lax.ppermute(tail, axis, [(i, (i + 1) % count) for i in range(ends)])  6.76 us
  transfers between devices with their start and end apart: 7, of which 6 were waited for; matrix products, arithmetic and copies ran while one was open for 3% of the time, Pallas kernels for 0%

commit v1 on v0

v1 whole, which is shorter than its diff:
```python
import functools
import math

import jax
import jax.numpy as jnp
from jax import lax
from jax.experimental import pallas as pl
from jax.experimental.pallas import tpu as pltpu
from jax.sharding import PartitionSpec as P

MEASURE_ROWS_MEAN = 16
ITERS = 2

screen = 0.3
current = 4.0

MESH = pl.DeviceIdType.MESH
F32 = jnp.float32
BF16 = jnp.bfloat16


def relax_weights(count):
    spread_half = 6.0 / (6.0 + screen)
    return [
        1.0 / (1.0 + spread_half * math.cos(math.pi * (2 * k + 1) / (2 * count)))
        for k in range(count)
    ]


def shifted(v, dim, step):
    size = v.shape[dim]
    index = lax.broadcasted_iota(jnp.int32, v.shape, dim)
    if step > 0:
        return jnp.where(index == 0, 0.0, pltpu.roll(v, 1, dim))
    return jnp.where(index == size - 1, 0.0, pltpu.roll(v, size - 1, dim))


def in_plane(v):
    return (
        shifted(v, 0, 1) + shifted(v, 0, -1) + shifted(v, 1, 1) + shifted(v, 1, -1)
    )


def kernel(
    n,
    spaces,
    slots,
    sig_r,
    sig_i,
    warm,
    loc,
    ints,
    out,
    pot,
    q,
    partial,
    halo_out,
    halo_in,
    gathered_ints,
    ints_smem,
    halo_send,
    halo_recv,
    ring_send,
    ring_recv,
    side_send,
    side_recv,
    int_send,
    int_recv,
    local_sem,
):
    half = n // 2
    w0, w1 = relax_weights(ITERS)
    elec = lax.axis_index("elec")
    space = lax.axis_index("space")
    even = lax.rem(elec, 2) == 0
    place = jnp.where(even, elec // 2, n - 1 - elec // 2)

    def elec_at(p):
        p = lax.rem(p + 2 * n, n)
        return jnp.where(p < half, 2 * p, 2 * (n - 1 - p) + 1)

    ahead, behind = elec_at(place + 1), elec_at(place - 1)
    has_left, has_right = space > 0, space < spaces - 1
    per = warm.shape[0]
    ny, nz = warm.shape[3], warm.shape[4]

    barrier = pltpu.get_barrier_semaphore()
    for o in range(1, n):
        pl.semaphore_signal(
            barrier, inc=1, device_id=(lax.rem(elec + o, n), space), device_id_type=MESH
        )

    @pl.when(has_left)
    def _():
        pl.semaphore_signal(barrier, inc=1, device_id=(elec, space - 1), device_id_type=MESH)

    @pl.when(has_right)
    def _():
        pl.semaphore_signal(barrier, inc=1, device_id=(elec, space + 1), device_id_type=MESH)

    for x in range(2):
        sr, si = sig_r[x], sig_i[x]
        inverse = current / ((6.0 + screen) * (sr * sr + si * si))
        q[0, x] = sr * inverse
        q[1, x] = -(si * inverse)

    y_index = lax.broadcasted_iota(jnp.int32, (ny, nz), 0)
    z_index = lax.broadcasted_iota(jnp.int32, (ny, nz), 1)
    cell = y_index * nz + z_index

    def source(e, part, x):
        flat = cell + (space * 2 + x) * (ny * nz)
        return jnp.where(flat == loc[e], q[part, x], 0.0)

    def first(i, carry):
        e = i // 2
        part = i - 2 * e
        for x in range(2):
            f = warm[e, part, x]
            other = warm[e, part, 1 - x]
            value = (
                (1.0 - w0) * f
                + w0 * source(e, part, x)
                + (w0 / (6.0 + screen)) * (in_plane(f) + other)
            )
            partial[i, x] = value
            halo_out[x, 0, i] = f.astype(BF16)
            halo_out[x, 1, i] = value.astype(BF16)
        return carry

    lax.fori_loop(0, 2 * per, first, 0)

    @pl.when(jnp.logical_not(has_left))
    def _():
        halo_in[0] = jnp.zeros(halo_in.shape[1:], BF16)
        for o in range(n):
            pot[o, 0] = jnp.zeros(pot.shape[2:], BF16)

    @pl.when(jnp.logical_not(has_right))
    def _():
        halo_in[1] = jnp.zeros(halo_in.shape[1:], BF16)
        for o in range(n):
            pot[o, 3] = jnp.zeros(pot.shape[2:], BF16)

    neighbours = jnp.where(has_left, 1, 0) + jnp.where(has_right, 1, 0)
    pl.semaphore_wait(barrier, n - 1 + neighbours)

    def warm_copy(side):
        return pltpu.make_async_remote_copy(
            src_ref=halo_out.at[side],
            dst_ref=halo_in.at[1 - side],
            send_sem=halo_send.at[side],
            recv_sem=halo_recv.at[1 - side],
            device_id=(elec, space - 1 if side == 0 else space + 1),
            device_id_type=MESH,
        )

    def warm_arrival(side):
        return pltpu.make_async_remote_copy(
            src_ref=halo_out.at[side],
            dst_ref=halo_in.at[side],
            send_sem=halo_send.at[side],
            recv_sem=halo_recv.at[side],
            device_id=(elec, space),
            device_id_type=MESH,
        )

    present = (has_left, has_right)
    for side in range(2):

        @pl.when(present[side])
        def _():
            warm_copy(side).start()

    def int_copy(o):
        return pltpu.make_async_remote_copy(
            src_ref=ints,
            dst_ref=gathered_ints.at[n - o],
            send_sem=int_send.at[o],
            recv_sem=int_recv.at[n - o],
            device_id=(lax.rem(elec + o, n), space),
            device_id_type=MESH,
        )

    for o in range(1, n):
        int_copy(o).start()

    for side in range(2):

        @pl.when(present[side])
        def _():
            warm_arrival(side).wait_recv()

    left_on = jnp.where(has_left, 1.0, 0.0).astype(F32)
    right_on = jnp.where(has_right, 1.0, 0.0).astype(F32)

    def second(i, carry):
        e = i // 2
        part = i - 2 * e
        c0 = w0 / (6.0 + screen)
        c1 = w1 / (6.0 + screen)
        warm_left = halo_in[0, 0, i].astype(F32)
        warm_right = halo_in[1, 0, i].astype(F32)
        low = partial[i, 0] + c0 * warm_left
        high = partial[i, 1] + c0 * warm_right
        left = halo_in[0, 1, i].astype(F32) + (c0 * left_on) * warm[e, part, 0]
        right = halo_in[1, 1, i].astype(F32) + (c0 * right_on) * warm[e, part, 1]
        pot[0, 1, i] = (
            (1.0 - w1) * low + w1 * source(e, part, 0) + c1 * (in_plane(low) + high + left)
        ).astype(BF16)
        pot[0, 2, i] = (
            (1.0 - w1) * high + w1 * source(e, part, 1) + c1 * (in_plane(high) + low + right)
        ).astype(BF16)
        return carry

    lax.fori_loop(0, 2 * per, second, 0)

    def ring_copy(way, o, x):
        src = o if way == 0 else (n - o) % n
        dst = o + 1 if way == 0 else n - o - 1
        return pltpu.make_async_remote_copy(
            src_ref=pot.at[src, 1 + x],
            dst_ref=pot.at[dst, 1 + x],
            send_sem=ring_send.at[way, o, x],
            recv_sem=ring_recv.at[way, o, x],
            device_id=(ahead if way == 0 else behind, space),
            device_id_type=MESH,
        )

    def side_copy(o, x):
        return pltpu.make_async_remote_copy(
            src_ref=pot.at[o, 1 + x],
            dst_ref=pot.at[o, 3 if x == 0 else 0],
            send_sem=side_send.at[o, x],
            recv_sem=side_recv.at[o, x],
            device_id=(elec, space - 1 if x == 0 else space + 1),
            device_id_type=MESH,
        )

    def send_side(o, x):
        @pl.when(present[x])
        def _():
            side_copy(o, x).start()

    def travels(way, o, x):
        return o < half - 1 or (o == half - 1 and x == way)

    for x in range(2):
        for way in range(2):
            if travels(way, 0, x):
                ring_copy(way, 0, x).start()
        send_side(0, x)
    for o in range(1, half + 1):
        for x in range(2):
            for way in range(2):
                if travels(way, o - 1, x):
                    ring_copy(way, o - 1, x).wait_recv()
                    if travels(way, o, x):
                        ring_copy(way, o, x).start()
                    send_side(o if way == 0 else n - o, x)

    for o in range(1, n):
        int_copy(n - o).wait_recv()
    gathered_ints[0] = ints[...]
    local = pltpu.make_async_copy(gathered_ints, ints_smem, local_sem)
    local.start()
    local.wait()

    for o in range(n):
        for x in range(2):

            @pl.when(present[1 - x])
            def _():
                side_copy(o, x).wait_recv()

    lanes = ints.shape[1]

    def row(r, carry):
        number = elec * MEASURE_ROWS_MEAN + r
        end = jnp.int32(0)
        start = jnp.int32(0)
        owner = jnp.int32(0)
        for g in range(n):
            where = lax.rem(g - elec + n, n)
            end = end + ints_smem[where, slots * 4 // lanes, slots * 4 % lanes]
            passed = end <= number
            owner = owner + jnp.where(passed, 1, 0)
            start = jnp.where(passed, end, start)
        slot = number - start
        where = lax.rem(owner - elec + n, n)

        def chosen(j):
            at = slot * 4 + j
            e = ints_smem[where, at // lanes, lax.rem(at, lanes)]
            h = e // per
            p = jnp.where(lax.rem(h, 2) == 0, h // 2, n - 1 - h // 2)
            return lax.rem(place - p + n, n), 2 * (e - h * per)

        picks = [chosen(j) for j in range(4)]

        def pair(k, part, x):
            (oa, ea), (ob, eb) = picks[2 * k], picks[2 * k + 1]
            return pot[oa, x, ea + part].astype(F32) - pot[ob, x, eb + part].astype(F32)

        for x in range(2):
            grads = []
            for k in range(2):
                parts = []
                for part in range(2):
                    v = pair(k, part, 1 + x)
                    parts.append(
                        (
                            pair(k, part, 2 + x) - pair(k, part, x),
                            shifted(v, 0, -1) - shifted(v, 0, 1),
                            shifted(v, 1, -1) - shifted(v, 1, 1),
                        )
                    )
                grads.append(parts)
            (s_re, s_im), (p_re, p_im) = grads
            dot_re = sum(s_re[c] * p_re[c] - s_im[c] * p_im[c] for c in range(3))
            dot_im = sum(s_re[c] * p_im[c] + s_im[c] * p_re[c] for c in range(3))
            sr, si = -0.25 * sig_r[x], -0.25 * sig_i[x]
            out[r, 0, x] = (sr * dot_re - si * dot_im).astype(BF16)
            out[r, 1, x] = (sr * dot_im + si * dot_re).astype(BF16)
        return carry

    lax.fori_loop(0, MEASURE_ROWS_MEAN, row, 0)

    for side in range(2):

        @pl.when(present[side])
        def _():
            warm_copy(side).wait_send()
            for o in range(n):
                side_copy(o, side).wait_send()

    for o in range(1, n):
        int_copy(o).wait_send()
    for o in range(half):
        for x in range(2):
            for way in range(2):
                if travels(way, o, x):
                    ring_copy(way, o, x).wait_send()


def per_device(n, spaces, sigma_real, sigma_imag, warm_fields, locations, counts, quads):
    per, parts, width, ny, nz = warm_fields.shape
    slots = quads.shape[1]
    fields = per * parts
    flat = jnp.concatenate([quads.reshape(-1), counts])
    flat = jnp.pad(flat, (0, 1024 - flat.shape[0])).reshape(8, 128)
    vmem = pl.BlockSpec(memory_space=pltpu.VMEM)
    smem = pl.BlockSpec(memory_space=pltpu.SMEM)
    half = n // 2
    dma = pltpu.SemaphoreType.DMA
    return pl.pallas_call(
        functools.partial(kernel, n, spaces, slots),
        out_shape=jax.ShapeDtypeStruct((MEASURE_ROWS_MEAN, 2, width, ny, nz), BF16),
        in_specs=[vmem, vmem, vmem, smem, vmem],
        out_specs=vmem,
        scratch_shapes=[
            pltpu.VMEM((n, width + 2, fields, ny, nz), BF16),
            pltpu.VMEM((2, width, ny, nz), F32),
            pltpu.VMEM((fields, width, ny, nz), F32),
            pltpu.VMEM((2, 2, fields, ny, nz), BF16),
            pltpu.VMEM((2, 2, fields, ny, nz), BF16),
            pltpu.VMEM((n, 8, 128), jnp.int32),
            pltpu.SMEM((n, 8, 128), jnp.int32),
            dma((2,)),
            dma((2,)),
            dma((2, half, 2)),
            dma((2, half, 2)),
            dma((n, 2)),
            dma((n, 2)),
            dma((n,)),
            dma((n,)),
            dma,
        ],
        compiler_params=pltpu.CompilerParams(
            collective_id=0, has_side_effects=True, vmem_limit_bytes=40 * 1024 * 1024
        ),
    )(sigma_real, sigma_imag, warm_fields, locations, flat)


def solution(mesh):
    in_specs = (
        P("space", None, None),
        P("space", None, None),
        P("elec", None, "space", None, None),
        P("elec"),
        P("elec"),
        P("elec", None, None),
    )
    out_specs = P("elec", None, "space", None, None)
    return jax.shard_map(
        functools.partial(per_device, mesh.shape["elec"], mesh.shape["space"]),
        mesh=mesh,
        in_specs=in_specs,
        out_specs=out_specs,
        check_vma=False,
    )
```

time: 179 us -> 48.1 us (0.27)
  waiting for transfers between devices: 69.9 us -> 0 us
  Pallas kernels: 0 us -> 41.9 us
  blocking collectives: 38.4 us -> 0 us
  local copies, waits for them, and re-layouts: 21.5 us -> 5.22 us
  starting transfers between devices: 14.2 us -> 0 us
  between operations: 14.3 us -> 0.67 us
  other arithmetic: 10.5 us -> 0.08 us
  matrix products: 8.32 us -> 0 us
    all_gather x1 -> x0, waiting for transfers between devices: 58.9 us -> none  [per_device(): gradient_table = lax.all_gather(own_grads, 'elec', axis=0, tiled=True)]
    pallas_call x0 -> x1, Pallas kernels: none -> 41.9 us  [per_device(): pl.pallas_call(functools.partial(kernel, n, spaces, slots), out_shape=jax...]
    all_gather x1 -> x0, blocking collectives: 26.7 us -> none  [per_device(): lax.all_gather(quads, 'elec', axis=0, tiled=True)]
    ppermute x6 -> x0, starting transfers between devices: 14.2 us -> none  [the longest x3 7.48 us: padded_2(): lax.ppermute(head, axis, [((i + 1) % count, i) for i in range(ends)])]
    unnamed x1 -> x0, blocking collectives: 11.7 us -> none
    ppermute x6 -> x0, waiting for transfers between devices: 11 us -> none  [the longest x3 7.76 us: padded_2(): lax.ppermute(tail, axis, [(i, (i + 1) % count) for i in range(ends)])]
    unnamed x14 -> x10, local copies, waits for them, and re-layouts: 14.5 us -> 5.11 us
    dot_general x1 -> x0, matrix products: 8.32 us -> none  [per_device(): jnp.dot(selector, gradient_table.reshape(electrodes, -1), preferred_eleme...]
  transfers between devices with their start and end apart: 7 -> 0, of which waited for: 6 -> 0; matrix products, arithmetic and copies ran while one was open for 3% -> 0% of each run, Pallas kernels for 0% -> 0%
where the time goes in v1:
time: 48.1 us; the launch traced here: 47.8 us
  Pallas kernels  41.9 us (87%)
  local copies, waits for them, and re-layouts  5.22 us (11%)
  between operations  0.67 us (1%)
    pallas_call x1, Pallas kernels, per_device(): pl.pallas_call(functools.partial(kernel, n, spaces, slots), out_shape=jax...  41.9 us
    unnamed x10, local copies, waits for them, and re-layouts  5.11 us

profile of v1, /device:TPU:2, one launch (start us, length us, event | category | flops | bytes accessed | tf_op | source)
XLA Modules:
  0.0 47.8 jit_solution(1161023512003186854)
XLA Ops:
  0.7 0.8 %copy.7 = s32[1,48,4]{2,1,0:T(8,128)S(1)} copy(s32[1,48,4]{1,2,0:T(4,128)} %param.11) | data formatting | bytes 1536 | tf_op args[5]
  1.4 0.1 reshape.6
  1.5 0.1 pad_add_fusion
  1.6 0.0 copy-start.3
  1.6 0.7 %copy-done.3 = s32[4]{0:T(128)S(1)} copy-done((s32[4]{0:T(128)S(1)}, s32[4]{0:T(128)}, u32[]{:S(2)}) %copy-start.3) | copy-done | bytes 40
  2.3 0.0 copy-start
  2.3 1.0 %copy-done = f32[4,2,2,64,128]{4,3,2,1,0:T(8,128)S(1)} copy-done((f32[4,2,2,64,128]{4,3,2,1,0:T(8,128)S(1)}, f32[4,2,2,64,128]{4,3,2,1,0:T(8,128)}, u32[]{:S(2)}) %copy-start) | copy-done | bytes 524312
  3.3 0.0 copy-start.1
  3.3 0.8 %copy-done.1 = f32[2,64,128]{2,1,0:T(8,128)S(1)} copy-done((f32[2,64,128]{2,1,0:T(8,128)S(1)}, f32[2,64,128]{2,1,0:T(8,128)}, u32[]{:S(2)}) %copy-start.1) | copy-done | bytes 65560
  4.1 0.0 copy-start.2
  4.1 0.8 %copy-done.2 = f32[2,64,128]{2,1,0:T(8,128)S(1)} copy-done((f32[2,64,128]{2,1,0:T(8,128)S(1)}, f32[2,64,128]{2,1,0:T(8,128)}, u32[]{:S(2)}) %copy-start.2) | copy-done | bytes 65560
  5.0 41.9 %shard_map.64 = bf16[16,2,2,64,128]{4,3,2,1,0:T(8,128)(2,1)S(1)} custom-call(f32[2,64,128]{2,1,0:T(8,128)S(1)} %copy-done.1, f32[2,64,128]{2,1,0:T(8,128)S(1)} %copy-done.2, f32[4,2,2,64,128]{4,3,2,1,0:T(8,128)S(1)} %copy-done, s32[4]{0:T(128)S(1)} %copy-done.3, s32[8,128]{1,0:T(8,128)S(1)} %pad_bitcast_fusion.ints), custom_call_target="tpu_custom_call" | custom-call | tf_op jit(solution)/shard_map/pallas_call | solution.py:356
  46.9 1.0 %copy.10 = bf16[16,2,2,64,128]{4,3,2,1,0:T(8,128)(2,1)} copy(bf16[16,2,2,64,128]{4,3,2,1,0:T(8,128)(2,1)S(1)} %shard_map.64) | data formatting | bytes 2097152
  (1 shorter events, 0.0 us)
Async XLA Ops:
  1.6 0.7 %copy-start.3 = (s32[4]{0:T(128)S(1)}, s32[4]{0:T(128)}, u32[]{:S(2)}) copy-start(s32[4]{0:T(128)} %loc.1) | copy-start | bytes 52
  2.3 1.0 %copy-start = (f32[4,2,2,64,128]{4,3,2,1,0:T(8,128)S(1)}, f32[4,2,2,64,128]{4,3,2,1,0:T(8,128)}, u32[]{:S(2)}) copy-start(f32[4,2,2,64,128]{4,3,2,1,0:T(8,128)} %warm.1) | copy-start | bytes 1572868
  3.3 0.8 %copy-start.1 = (f32[2,64,128]{2,1,0:T(8,128)S(1)}, f32[2,64,128]{2,1,0:T(8,128)}, u32[]{:S(2)}) copy-start(f32[2,64,128]{2,1,0:T(8,128)} %sig_r.1) | copy-start | bytes 196612
  4.1 0.8 %copy-start.2 = (f32[2,64,128]{2,1,0:T(8,128)S(1)}, f32[2,64,128]{2,1,0:T(8,128)}, u32[]{:S(2)}) copy-start(f32[2,64,128]{2,1,0:T(8,128)} %sig_i.1) | copy-start | bytes 196612

commit v2 on v1

--- a/solution.py
+++ b/solution.py
@@ -45,12 +45,18 @@
     n,
     spaces,
     slots,
+    sig_r_hbm,
+    sig_i_hbm,
+    warm_hbm,
+    quads_hbm,
+    loc,
+    count,
+    out,
     sig_r,
     sig_i,
     warm,
-    loc,
+    quads,
     ints,
-    out,
     pot,
     q,
     partial,
@@ -58,6 +64,9 @@
     halo_in,
     gathered_ints,
     ints_smem,
+    picks,
+    table,
+    rows_out,
     halo_send,
     halo_recv,
     ring_send,
@@ -66,7 +75,9 @@
     side_recv,
     int_send,
     int_recv,
+    load_sem,
     local_sem,
+    out_sem,
 ):
     half = n // 2
     w0, w1 = relax_weights(ITERS)
@@ -84,6 +95,15 @@
     per = warm.shape[0]
     ny, nz = warm.shape[3], warm.shape[4]
 
+    loads = [
+        pltpu.make_async_copy(a, b, load_sem.at[k])
+        for k, (a, b) in enumerate(
+            [(warm_hbm, warm), (sig_r_hbm, sig_r), (sig_i_hbm, sig_i), (quads_hbm, quads)]
+        )
+    ]
+    for load in loads:
+        load.start()
+
     barrier = pltpu.get_barrier_semaphore()
     for o in range(1, n):
         pl.semaphore_signal(
@@ -97,6 +117,24 @@
     @pl.when(has_right)
     def _():
         pl.semaphore_signal(barrier, inc=1, device_id=(elec, space + 1), device_id_type=MESH)
+
+    @pl.when(jnp.logical_not(has_left))
+    def _():
+        halo_in[0] = jnp.zeros(halo_in.shape[1:], BF16)
+        for o in range(n):
+            pot[o, 0] = jnp.zeros(pot.shape[2:], BF16)
+
+    @pl.when(jnp.logical_not(has_right))
+    def _():
+        halo_in[1] = jnp.zeros(halo_in.shape[1:], BF16)
+        for o in range(n):
+            pot[o, 3] = jnp.zeros(pot.shape[2:], BF16)
+
+    for load in loads:
+        load.wait()
+    ints[...] = jnp.zeros(ints.shape, jnp.int32)
+    ints[0:4, 0:slots] = quads[0]
+    ints[4:5, :] = jnp.full((1, ints.shape[1]), count[0], jnp.int32)
 
     for x in range(2):
         sr, si = sig_r[x], sig_i[x]
@@ -129,18 +167,6 @@
         return carry
 
     lax.fori_loop(0, 2 * per, first, 0)
-
-    @pl.when(jnp.logical_not(has_left))
-    def _():
-        halo_in[0] = jnp.zeros(halo_in.shape[1:], BF16)
-        for o in range(n):
-            pot[o, 0] = jnp.zeros(pot.shape[2:], BF16)
-
-    @pl.when(jnp.logical_not(has_right))
-    def _():
-        halo_in[1] = jnp.zeros(halo_in.shape[1:], BF16)
-        for o in range(n):
-            pot[o, 3] = jnp.zeros(pot.shape[2:], BF16)
 
     neighbours = jnp.where(has_left, 1, 0) + jnp.where(has_right, 1, 0)
     pl.semaphore_wait(barrier, n - 1 + neighbours)
@@ -245,11 +271,63 @@
     def travels(way, o, x):
         return o < half - 1 or (o == half - 1 and x == way)
 
+    def wait_sides(o):
+        for x in range(2):
+
+            @pl.when(present[1 - x])
+            def _():
+                side_copy(o, x).wait_recv()
+
+    def gradients(o):
+        def one(i, carry):
+            planes = [pot[o, k, i].astype(F32) for k in range(4)]
+            for x in range(2):
+                v = planes[1 + x]
+                table[o, i, x, 0] = ((planes[2 + x] - planes[x]) * 0.5).astype(BF16)
+                table[o, i, x, 1] = ((shifted(v, 0, -1) - shifted(v, 0, 1)) * 0.5).astype(BF16)
+                table[o, i, x, 2] = ((shifted(v, 1, -1) - shifted(v, 1, 1)) * 0.5).astype(BF16)
+            return carry
+
+        lax.fori_loop(0, 2 * per, one, 0)
+
+    def choose(r, carry):
+        number = elec * MEASURE_ROWS_MEAN + r
+        end = jnp.int32(0)
+        start = jnp.int32(0)
+        owner = jnp.int32(0)
+        for g in range(n):
+            where = lax.rem(g - elec + n, n)
+            end = end + ints_smem[where, 4, 0]
+            passed = end <= number
+            owner = owner + jnp.where(passed, 1, 0)
+            start = jnp.where(passed, end, start)
+        slot = number - start
+        where = lax.rem(owner - elec + n, n)
+        for j in range(4):
+            e = ints_smem[where, j, slot]
+            h = e // per
+            p = jnp.where(lax.rem(h, 2) == 0, h // 2, n - 1 - h // 2)
+            picks[r, 2 * j] = lax.rem(place - p + n, n)
+            picks[r, 2 * j + 1] = 2 * (e - h * per)
+        return carry
+
+    def row_copy(r):
+        return pltpu.make_async_copy(rows_out.at[r], out.at[r], out_sem.at[r])
+
     for x in range(2):
         for way in range(2):
             if travels(way, 0, x):
                 ring_copy(way, 0, x).start()
         send_side(0, x)
+
+    for o in range(1, n):
+        int_copy(n - o).wait_recv()
+    gathered_ints[0] = ints[...]
+    local = pltpu.make_async_copy(gathered_ints, ints_smem, local_sem)
+    local.start()
+    local.wait()
+    lax.fori_loop(0, MEASURE_ROWS_MEAN, choose, 0)
+
     for o in range(1, half + 1):
         for x in range(2):
             for way in range(2):
@@ -258,70 +336,31 @@
                     if travels(way, o, x):
                         ring_copy(way, o, x).start()
                     send_side(o if way == 0 else n - o, x)
-
-    for o in range(1, n):
-        int_copy(n - o).wait_recv()
-    gathered_ints[0] = ints[...]
-    local = pltpu.make_async_copy(gathered_ints, ints_smem, local_sem)
-    local.start()
-    local.wait()
-
-    for o in range(n):
+        for done in sorted({o - 1, (n - o + 1) % n}):
+            wait_sides(done)
+            gradients(done)
+
+    wait_sides(half)
+    gradients(half)
+
+    def row(r, carry):
+        at = [(picks[r, 2 * j], picks[r, 2 * j + 1]) for j in range(4)]
+
+        def pair(k, part, x, c):
+            (oa, ea), (ob, eb) = at[2 * k], at[2 * k + 1]
+            return table[oa, ea + part, x, c].astype(F32) - table[ob, eb + part, x, c].astype(F32)
+
         for x in range(2):
-
-            @pl.when(present[1 - x])
-            def _():
-                side_copy(o, x).wait_recv()
-
-    lanes = ints.shape[1]
-
-    def row(r, carry):
-        number = elec * MEASURE_ROWS_MEAN + r
-        end = jnp.int32(0)
-        start = jnp.int32(0)
-        owner = jnp.int32(0)
-        for g in range(n):
-            where = lax.rem(g - elec + n, n)
-            end = end + ints_smem[where, slots * 4 // lanes, slots * 4 % lanes]
-            passed = end <= number
-            owner = owner + jnp.where(passed, 1, 0)
-            start = jnp.where(passed, end, start)
-        slot = number - start
-        where = lax.rem(owner - elec + n, n)
-
-        def chosen(j):
-            at = slot * 4 + j
-            e = ints_smem[where, at // lanes, lax.rem(at, lanes)]
-            h = e // per
-            p = jnp.where(lax.rem(h, 2) == 0, h // 2, n - 1 - h // 2)
-            return lax.rem(place - p + n, n), 2 * (e - h * per)
-
-        picks = [chosen(j) for j in range(4)]
-
-        def pair(k, part, x):
-            (oa, ea), (ob, eb) = picks[2 * k], picks[2 * k + 1]
-            return pot[oa, x, ea + part].astype(F32) - pot[ob, x, eb + part].astype(F32)
-
-        for x in range(2):
-            grads = []
-            for k in range(2):
-                parts = []
-                for part in range(2):
-                    v = pair(k, part, 1 + x)
-                    parts.append(
-                        (
-                            pair(k, part, 2 + x) - pair(k, part, x),
-                            shifted(v, 0, -1) - shifted(v, 0, 1),
-                            shifted(v, 1, -1) - shifted(v, 1, 1),
-                        )
-                    )
-                grads.append(parts)
-            (s_re, s_im), (p_re, p_im) = grads
-            dot_re = sum(s_re[c] * p_re[c] - s_im[c] * p_im[c] for c in range(3))
-            dot_im = sum(s_re[c] * p_im[c] + s_im[c] * p_re[c] for c in range(3))
-            sr, si = -0.25 * sig_r[x], -0.25 * sig_i[x]
-            out[r, 0, x] = (sr * dot_re - si * dot_im).astype(BF16)
-            out[r, 1, x] = (sr * dot_im + si * dot_re).astype(BF16)
+            dot_re = dot_im = 0.0
+            for c in range(3):
+                s_re, s_im = pair(0, 0, x, c), pair(0, 1, x, c)
+                p_re, p_im = pair(1, 0, x, c), pair(1, 1, x, c)
+                dot_re = dot_re + (s_re * p_re - s_im * p_im)
+                dot_im = dot_im + (s_re * p_im + s_im * p_re)
+            sr, si = sig_r[x], sig_i[x]
+            rows_out[r, 0, x] = (si * dot_im - sr * dot_re).astype(BF16)
+            rows_out[r, 1, x] = (-(sr * dot_im + si * dot_re)).astype(BF16)
+        row_copy(r).start()
         return carry
 
     lax.fori_loop(0, MEASURE_ROWS_MEAN, row, 0)
@@ -342,23 +381,32 @@
                 if travels(way, o, x):
                     ring_copy(way, o, x).wait_send()
 
+    def finish(r, carry):
+        row_copy(r).wait()
+        return carry
+
+    lax.fori_loop(0, MEASURE_ROWS_MEAN, finish, 0)
+
 
 def per_device(n, spaces, sigma_real, sigma_imag, warm_fields, locations, counts, quads):
     per, parts, width, ny, nz = warm_fields.shape
     slots = quads.shape[1]
     fields = per * parts
-    flat = jnp.concatenate([quads.reshape(-1), counts])
-    flat = jnp.pad(flat, (0, 1024 - flat.shape[0])).reshape(8, 128)
-    vmem = pl.BlockSpec(memory_space=pltpu.VMEM)
+    hbm = pl.BlockSpec(memory_space=pltpu.HBM)
     smem = pl.BlockSpec(memory_space=pltpu.SMEM)
     half = n // 2
     dma = pltpu.SemaphoreType.DMA
     return pl.pallas_call(
         functools.partial(kernel, n, spaces, slots),
         out_shape=jax.ShapeDtypeStruct((MEASURE_ROWS_MEAN, 2, width, ny, nz), BF16),
-        in_specs=[vmem, vmem, vmem, smem, vmem],
-        out_specs=vmem,
+        in_specs=[hbm, hbm, hbm, hbm, smem, smem],
+        out_specs=hbm,
         scratch_shapes=[
+            pltpu.VMEM((width, ny, nz), F32),
+            pltpu.VMEM((width, ny, nz), F32),
+            pltpu.VMEM(warm_fields.shape, F32),
+            pltpu.VMEM((1, 4, slots), jnp.int32),
+            pltpu.VMEM((8, 128), jnp.int32),
             pltpu.VMEM((n, width + 2, fields, ny, nz), BF16),
             pltpu.VMEM((2, width, ny, nz), F32),
             pltpu.VMEM((fields, width, ny, nz), F32),
@@ -366,6 +414,9 @@
             pltpu.VMEM((2, 2, fields, ny, nz), BF16),
             pltpu.VMEM((n, 8, 128), jnp.int32),
             pltpu.SMEM((n, 8, 128), jnp.int32),
+            pltpu.SMEM((MEASURE_ROWS_MEAN, 8), jnp.int32),
+            pltpu.VMEM((n, fields, width, 3, ny, nz), BF16),
+            pltpu.VMEM((MEASURE_ROWS_MEAN, 2, width, ny, nz), BF16),
             dma((2,)),
             dma((2,)),
             dma((2, half, 2)),
@@ -374,12 +425,14 @@
             dma((n, 2)),
             dma((n,)),
             dma((n,)),
+            dma((4,)),
             dma,
+            dma((MEASURE_ROWS_MEAN,)),
         ],
         compiler_params=pltpu.CompilerParams(
-            collective_id=0, has_side_effects=True, vmem_limit_bytes=40 * 1024 * 1024
+            collective_id=0, has_side_effects=True, vmem_limit_bytes=60 * 1024 * 1024
         ),
-    )(sigma_real, sigma_imag, warm_fields, locations, flat)
+    )(sigma_real, sigma_imag, warm_fields, quads.transpose(0, 2, 1), locations, counts)
 
 
 def solution(mesh):

time: 48.1 us -> 43.4 us (0.902)
  local copies, waits for them, and re-layouts: 5.22 us -> 2.31 us
  Pallas kernels: 41.9 us -> 40.2 us
    unnamed x10 -> x1, local copies, waits for them, and re-layouts: 5.11 us -> 2.31 us
    pallas_call x1, Pallas kernels: 41.9 us -> 40.2 us  [per_device(): pl.pallas_call(functools.partial(kernel, n, spaces, slots), out_shape=jax...]
where the time goes in v2:
time: 43.4 us; the launch traced here: 43.2 us
  Pallas kernels  40.2 us (93%)
  local copies, waits for them, and re-layouts  2.31 us (5%)
  between operations  0.66 us (2%)
    pallas_call x1, Pallas kernels, per_device(): pl.pallas_call(functools.partial(kernel, n, spaces, slots), out_shape=jax...  40.2 us
    unnamed x1, local copies, waits for them, and re-layouts  2.31 us

profile of v2, /device:TPU:2, one launch (start us, length us, event | category | flops | bytes accessed | tf_op | source)
XLA Modules:
  0.0 43.2 jit_solution(14181181724592569096)
XLA Ops:
  0.7 40.2 %shard_map.64 = bf16[16,2,2,64,128]{4,3,2,1,0:T(8,128)(2,1)} custom-call(f32[2,64,128]{2,1,0:T(8,128)} %sig_r_hbm.1, f32[2,64,128]{2,1,0:T(8,128)} %sig_i_hbm.1, f32[4,2,2,64,128]{4,3,2,1,0:T(8,128)} %warm_hbm.1, s32[1,4,48]{2,1,0:T(4,128)} %bitcast.1, s32[4]{0:T(128)} %loc.1, s32[1]{0:T(128)S(6)} %copy.8.count), custom_call_target="tpu_custom_call" | custom-call | tf_op jit(solution)/shard_map/pallas_call | solution.py:399
  40.9 2.3 %copy.9 = bf16[16,2,2,64,128]{4,3,2,1,0:T(8,128)(2,1)} copy(bf16[16,2,2,64,128]{4,3,2,1,0:T(8,128)(2,1)} %shard_map.64) | data formatting | bytes 2097152

commit v3 on v2

--- a/solution.py
+++ b/solution.py
@@ -66,7 +66,6 @@
     ints_smem,
     picks,
     table,
-    rows_out,
     halo_send,
     halo_recv,
     ring_send,
@@ -77,7 +76,6 @@
     int_recv,
     load_sem,
     local_sem,
-    out_sem,
 ):
     half = n // 2
     w0, w1 = relax_weights(ITERS)
@@ -311,9 +309,6 @@
             picks[r, 2 * j + 1] = 2 * (e - h * per)
         return carry
 
-    def row_copy(r):
-        return pltpu.make_async_copy(rows_out.at[r], out.at[r], out_sem.at[r])
-
     for x in range(2):
         for way in range(2):
             if travels(way, 0, x):
@@ -358,9 +353,8 @@
                 dot_re = dot_re + (s_re * p_re - s_im * p_im)
                 dot_im = dot_im + (s_re * p_im + s_im * p_re)
             sr, si = sig_r[x], sig_i[x]
-            rows_out[r, 0, x] = (si * dot_im - sr * dot_re).astype(BF16)
-            rows_out[r, 1, x] = (-(sr * dot_im + si * dot_re)).astype(BF16)
-        row_copy(r).start()
+            out[r, 0, x] = (si * dot_im - sr * dot_re).astype(BF16)
+            out[r, 1, x] = (-(sr * dot_im + si * dot_re)).astype(BF16)
         return carry
 
     lax.fori_loop(0, MEASURE_ROWS_MEAN, row, 0)
@@ -380,12 +374,6 @@
             for way in range(2):
                 if travels(way, o, x):
                     ring_copy(way, o, x).wait_send()
-
-    def finish(r, carry):
-        row_copy(r).wait()
-        return carry
-
-    lax.fori_loop(0, MEASURE_ROWS_MEAN, finish, 0)
 
 
 def per_device(n, spaces, sigma_real, sigma_imag, warm_fields, locations, counts, quads):
@@ -398,9 +386,9 @@
     dma = pltpu.SemaphoreType.DMA
     return pl.pallas_call(
         functools.partial(kernel, n, spaces, slots),
-        out_shape=jax.ShapeDtypeStruct((MEASURE_ROWS_MEAN, 2, width, ny, nz), BF16),
+        out_shape=pltpu.VMEM((MEASURE_ROWS_MEAN, 2, width, ny, nz), BF16),
         in_specs=[hbm, hbm, hbm, hbm, smem, smem],
-        out_specs=hbm,
+        out_specs=pl.BlockSpec(memory_space=pltpu.VMEM),
         scratch_shapes=[
             pltpu.VMEM((width, ny, nz), F32),
             pltpu.VMEM((width, ny, nz), F32),
@@ -416,7 +404,6 @@
             pltpu.SMEM((n, 8, 128), jnp.int32),
             pltpu.SMEM((MEASURE_ROWS_MEAN, 8), jnp.int32),
             pltpu.VMEM((n, fields, width, 3, ny, nz), BF16),
-            pltpu.VMEM((MEASURE_ROWS_MEAN, 2, width, ny, nz), BF16),
             dma((2,)),
             dma((2,)),
             dma((2, half, 2)),
@@ -427,7 +414,6 @@
             dma((n,)),
             dma((4,)),
             dma,
-            dma((MEASURE_ROWS_MEAN,)),
         ],
         compiler_params=pltpu.CompilerParams(
             collective_id=0, has_side_effects=True, vmem_limit_bytes=60 * 1024 * 1024

time: 43.4 us -> 41.3 us (0.952)
  local copies, waits for them, and re-layouts: 2.31 us -> 0.97 us
  Pallas kernels: 40.2 us -> 39.5 us
    unnamed x1, local copies, waits for them, and re-layouts: 2.31 us -> 0.97 us
    pallas_call x1, Pallas kernels: 40.2 us -> 39.5 us  [per_device(): pl.pallas_call(functools.partial(kernel, n, spaces, slots), out_shape=plt...]
where the time goes in v3:
time: 41.3 us; the launch traced here: 41.1 us
  Pallas kernels  39.5 us (96%)
  local copies, waits for them, and re-layouts  0.97 us (2%)
  between operations  0.66 us (2%)
    pallas_call x1, Pallas kernels, per_device(): pl.pallas_call(functools.partial(kernel, n, spaces, slots), out_shape=plt...  39.5 us
    unnamed x1, local copies, waits for them, and re-layouts  0.97 us

profile of v3, /device:TPU:2, one launch (start us, length us, event | category | flops | bytes accessed | tf_op | source)
XLA Modules:
  0.0 41.1 jit_solution(4842403173985108470)
XLA Ops:
  0.7 39.5 %shard_map.64 = bf16[16,2,2,64,128]{4,3,2,1,0:T(8,128)(2,1)S(1)} custom-call(f32[2,64,128]{2,1,0:T(8,128)} %sig_r_hbm.1, f32[2,64,128]{2,1,0:T(8,128)} %sig_i_hbm.1, f32[4,2,2,64,128]{4,3,2,1,0:T(8,128)} %warm_hbm.1, s32[1,4,48]{2,1,0:T(4,128)} %bitcast.1, s32[4]{0:T(128)} %loc.1, s32[1]{0:T(128)S(6)} %copy.9.count), custom_call_target="tpu_custom_call" | custom-call | tf_op jit(solution)/shard_map/pallas_call | solution.py:387
  40.2 1.0 %copy.8 = bf16[16,2,2,64,128]{4,3,2,1,0:T(8,128)(2,1)} copy(bf16[16,2,2,64,128]{4,3,2,1,0:T(8,128)(2,1)S(1)} %shard_map.64) | data formatting | bytes 2097152
